TPU v7x, 1024 devices: a whole 4x4x32 slice. The times are simulated.
1024 devices in a mesh: dp: 128 (over z, x), vocab: 8 (over y, core).
Axes of the slice: x: 4, y: 4, z: 32, core: 2. Of those that a mesh axis runs over, the one named last changes fastest.
Arguments:
- hidden: bfloat16 [24576, 4608], P('dp')
- table: bfloat16 [768, 4608], P('vocab')
- targets: int32 [24576], P('dp'), may hold values from 0 to 767
- loss_weight: float32 [24576], P('dp'), may hold values from 1 to 4
- token_ids: int32 [24576], P(('dp', 'vocab')), may hold values from 0 to 767, as said below
- grad_embed: bfloat16 [24576, 4608], P(('dp', 'vocab')), may hold values from -0.0234375 to 0.0234375
Outputs:
- token_loss: float32 [24576], P('dp')
- input_grad: bfloat16 [24576, 4608], P(('dp', 'vocab'))
- table_grad: bfloat16 [8, 3456, 128], P('vocab', 'dp')
Inputs may be any that keep to these rules, and one draw needn't show every extreme that they name: `token_ids`: the rows of each device along dp+vocab (aligned blocks of 24) name ids of any one vocabulary block of 96 entries at most 12 times; in every group of devices along vocab all devices name exactly 12 ids of one common block.
All inputs are finite; a program needn't handle non-finite values.
Results may differ from a plain program's by a relative error of at most 0.014.
Values may be sent and summed in bfloat16 or wider, within the bound.
A program may use at most 32 MiB of HBM per device.

v0:
```python
import math

import jax
import jax.numpy as jnp
from jax import lax
from jax.sharding import PartitionSpec as P

SOFTCAP = 30.0


def body(hidden, table, targets, loss_weight, token_ids, grad_embed):
    entries = table.shape[0]
    width = table.shape[1]
    shard_count = lax.axis_size("vocab")
    my_shard = lax.axis_index("vocab")
    rows_here = token_ids.shape[0]
    capacity = rows_here // 2
    raw_logits = lax.dot_general(
        hidden, table, (((1,), (1,)), ((), ())), preferred_element_type=jnp.float32
    )
    squashed = jnp.tanh(raw_logits / SOFTCAP)
    capped = SOFTCAP * squashed
    exponent = jnp.exp(capped)
    columns = jnp.arange(entries, dtype=jnp.int32)
    target_hit = (targets - my_shard * entries)[:, None] == columns[None, :]
    normalizer, picked = lax.psum(
        (jnp.sum(exponent, axis=1), jnp.sum(jnp.where(target_hit, capped, 0.0), axis=1)), "vocab"
    )
    token_loss = jnp.log(normalizer) - picked
    dlogit = (
        loss_weight[:, None]
        * (exponent / normalizer[:, None] - target_hit.astype(jnp.float32))
        * (1.0 - squashed * squashed)
    ).astype(jnp.bfloat16)
    input_grad = lax.psum_scatter(
        jnp.dot(dlogit, table, preferred_element_type=jnp.float32).astype(jnp.bfloat16),
        "vocab",
        scatter_dimension=0,
        tiled=True,
    )
    owner_shard = token_ids // entries
    local_id = token_ids % entries
    shard_range = jnp.arange(shard_count, dtype=jnp.int32)
    member = (owner_shard[:, None] == shard_range[None, :]).astype(jnp.int32)
    slot_rank = jnp.sum(jnp.cumsum(member, axis=0) * member, axis=1) - 1
    chosen = (owner_shard[None, None, :] == shard_range[:, None, None]) & (
        slot_rank[None, None, :] == jnp.arange(capacity, dtype=jnp.int32)[None, :, None]
    )
    outgoing = jnp.einsum(
        "bcr,rd->bcd", chosen.astype(jnp.bfloat16), grad_embed, preferred_element_type=jnp.float32
    ).astype(jnp.bfloat16)
    slot_ids = jnp.sum(jnp.where(chosen, local_id[None, None, :] + 1, 0), axis=2) - 1
    arrived, arrived_ids = (
        lax.all_to_all(outgoing, "vocab", split_axis=0, concat_axis=0, tiled=True),
        lax.all_to_all(slot_ids, "vocab", split_axis=0, concat_axis=0, tiled=True),
    )
    arrived = arrived.reshape(shard_count * capacity, width)
    arrived_ids = arrived_ids.reshape(shard_count * capacity)
    embed_scale = math.sqrt(width)
    head_part = lax.dot_general(
        dlogit, hidden, (((0,), (0,)), ((), ())), preferred_element_type=jnp.float32
    )
    wanted = (arrived_ids[None, :] == columns[:, None]).astype(jnp.bfloat16)
    embed_part = jnp.dot(wanted, arrived, preferred_element_type=jnp.float32)
    table_term = (head_part + embed_scale * embed_part).reshape(entries * width // 128, 128)
    group_count = lax.axis_size("dp")
    line_count = table_term.shape[0] // group_count
    summed_all = lax.psum(table_term, "dp")
    owned_lines = lax.dynamic_slice_in_dim(
        summed_all, lax.axis_index("dp") * line_count, line_count, 0
    )
    table_grad = owned_lines.astype(jnp.bfloat16)[None]
    return (token_loss, input_grad, table_grad)


def solution(mesh):
    return jax.shard_map(
        body,
        mesh=mesh,
        in_specs=(
            P("dp", None),
            P("vocab", None),
            P("dp"),
            P("dp"),
            P(("dp", "vocab")),
            P(("dp", "vocab"), None),
        ),
        out_specs=(P("dp"), P(("dp", "vocab"), None), P("vocab", "dp", None)),
        check_vma=False,
    )
```

profile of v0, /device:TPU:6, one launch (start us, length us, event | category | flops | bytes accessed | tf_op | source)
XLA Modules:
  0.0 648.4 jit_solution(16074964987170134009)
XLA Ops:
  7.3 0.8 broadcast_subtract_fusion
  8.1 0.6 copy-done
  8.7 1.9 exponential_reduce_fusion
  10.6 14.9 %all-reduce = (f32[192]{0:T(256)S(1)}, f32[192]{0:T(256)S(1)}) all-reduce(f32[192]{0:T(256)S(1)} %get-tuple-element.4, f32[192]{0:T(256)S(1)} %get-tuple-element.3), channel_id=1, replica_groups=mesh['dp'=128,'vocab'=8] {'vocab'}, use_global_device_ids=true, to_apply=%region_3.4 | all-reduce | flops 384 | bytes 3072 | tf_op jit(solution)/shard_map/psum | solution.py:26
  25.4 1.9 convolution_convert_fusion
  27.4 0.1 fusion.8
  27.5 0.2 select_reduce_fusion.1
  27.7 0.2 fusion.4
  27.9 0.6 broadcast_add_fusion
  28.5 3.3 all-to-all-start
  31.9 1.5 convolution_convert_fusion.1
  33.3 3.6 all-to-all-done
  37.0 3.6 all-to-all-start.1
  40.5 0.6 log_subtract_fusion
  41.1 1.6 fusion.11
  42.7 0.5 broadcast.91
  43.2 0.7 reduce.3
  43.9 0.1 eq.91
  44.0 13.9 %all-to-all-done.1 = bf16[8,12,4608]{2,1,0:T(8,128)(2,1)S(1)} async-done(((bf16[8,12,4608]{2,1,0:T(8,128)(2,1)}), bf16[8,12,4608]{2,1,0:T(8,128)(2,1)S(1)}, u32[]{:S(2)}, u32[]{:S(2)}) %all-to-all-start.1) | async-done | bytes 884768 | tf_op jit(solution)/shard_map/all_to_all | solution.py:54
  57.8 1.1 reshape.79
  59.0 2.2 fusion
  61.1 1.3 reshape.80
  62.4 578.5 %all-reduce.2 = bf16[3456,128]{1,0:T(8,128)(2,1)S(1)} all-reduce(f32[3456,128]{1,0:T(8,128)} %reshape.80), channel_id=1, replica_groups=mesh['dp'=128,'vocab'=8] {'dp'}, use_global_device_ids=true, to_apply=%region_8.9 | all-reduce | flops 442368 | bytes 2654208 | tf_op jit(solution)/shard_map/psum | solution.py:68
  641.0 0.6 fusion.9
  (17 shorter events, 0.2 us)
Async XLA Ops:
  7.2 1.5 copy-start
  7.2 18.2 %copy-start.1 = (bf16[96,4608]{1,0:T(8,128)(2,1)S(1)}, bf16[96,4608]{1,0:T(8,128)(2,1)}, u32[]{:S(2)}) copy-start(bf16[96,4608]{1,0:T(8,128)(2,1)} %param.7) | copy-start | bytes 2654212
  7.2 18.2 %copy-start.3 = (f32[192]{0:T(256)S(1)}, f32[192]{0:T(256)}, u32[]{:S(2)}) copy-start(f32[192]{0:T(256)} %param.9) | copy-start | bytes 2308
  7.2 634.4 %reduce-scatter.2.cloned.1.call-start = ((), (), s32[]{:S(2)}) async-start(), calls=%async_computation.3 | async-start | bytes 1990656 | tf_op jit(solution)/shard_map/reduce_scatter | solution.py:35
  25.4 1.9 copy-start.4
  25.4 6.4 copy-start.2
  28.5 8.4 %all-to-all-start = ((s32[8,1,12]{2,1,0:T(1,128)}), s32[8,1,12]{2,1,0:T(1,128)S(1)}, u32[]{:S(2)}, u32[]{:S(2)}) async-start(s32[8,1,12]{2,1,0:T(1,128)} %bitcast.1), calls=%async_computation.1 | async-start | bytes 8192 | tf_op jit(solution)/shard_map/all_to_all | solution.py:55
  37.0 20.9 %all-to-all-start.1 = ((bf16[8,12,4608]{2,1,0:T(8,128)(2,1)}), bf16[8,12,4608]{2,1,0:T(8,128)(2,1)S(1)}, u32[]{:S(2)}, u32[]{:S(2)}) async-start(bf16[8,12,4608]{2,1,0:T(8,128)(2,1)} %convolution_convert_fusion.1), calls=%async_computation.2 | async-start | bytes 2359296 | tf_op jit(solution)/shard_map/all_to_all | solution.py:54
Sparse Core Ops, SparseCore 0:
  27.5 55.7 reduce-scatter.1
where the time goes:
time: 657 us; the launch traced here: 648 us
  blocking collectives  593 us (90%)
  waiting for transfers between devices  17.5 us (3%)
  between operations  14.2 us (2%)
  matrix products  9 us (1%)
  starting transfers between devices  6.91 us (1%)
    psum x1, blocking collectives, body(): summed_all = lax.psum(table_term, 'dp')  579 us
    psum x1, blocking collectives, body(): lax.psum((jnp.sum(exponent, axis=1), jnp.sum(jnp.where(target_hit, capped...  14.9 us
    all_to_all x1, waiting for transfers between devices, body(): lax.all_to_all(outgoing, 'vocab', split_axis=0, concat_axis=0, tiled=True)  13.9 us
  transfers between devices with their start and end apart: 3, of which 2 were waited for; matrix products, arithmetic and copies ran while one was open for 2% of the time, Pallas kernels for 0%

commit v1 on v0

v1 whole, which is shorter than its diff:
```python
import functools
import math

import jax
import jax.numpy as jnp
from jax import lax
from jax.experimental import pallas as pl
from jax.experimental.pallas import tpu as pltpu
from jax.sharding import PartitionSpec as P

MESH = pl.DeviceIdType.MESH
SOFTCAP = 30.0
F32 = jnp.float32
BF16 = jnp.bfloat16

D = 4608
ENT = 96
TOK = 192
ROWS = 24
QUARTER = D // 4
PAIR = 2 * ROWS
HALF = 1792
STEP = 384
NX, NY, NZ, NC = 4, 4, 32, 2


def nt(a, b):
    return lax.dot_general(a, b, (((1,), (1,)), ((), ())), preferred_element_type=F32)


def tn(a, b):
    return lax.dot_general(a, b, (((0,), (0,)), ((), ())), preferred_element_type=F32)


def nn(a, b):
    return jnp.dot(a, b, preferred_element_type=F32)


def kernel(
    hidden_hbm, table_hbm, embed_hbm, targets_ref, weight_ref, ids_ref,
    loss_ref, input_ref, table_grad_ref,
    hid, tab, emb_in, emb, stats, xs, xown, xr, acc, ig_core, ig_core_in, ig_own, ig_y, ig_y_in,
    units, zf, zs, zr1, zb, zm, zr2,
    load_sem, emb_s, emb_r, fwd_s, fwd_r, st_s, st_r, x_s, x_r, c_s, c_r, y_s, y_r, z1_s, z1_r, z2_s, z2_r,
):
    dp = lax.axis_index("dp")
    vocab = lax.axis_index("vocab")
    z, x = dp // NX, lax.rem(dp, NX)
    y, core = vocab // NC, lax.rem(vocab, NC)
    slot = core * NY + y

    def at(dz=0, dx=0, dy=0, dc=0):
        zz, xx = lax.rem(z + dz + NZ, NZ), lax.rem(x + dx + NX, NX)
        yy, cc = lax.rem(y + dy + NY, NY), lax.rem(core + dc, NC)
        return (zz * NX + xx, yy * NC + cc)

    def remote(src, dst, send, recv, device):
        return pltpu.make_async_remote_copy(
            src_ref=src, dst_ref=dst, send_sem=send, recv_sem=recv, device_id=device, device_id_type=MESH
        )

    loads = [
        pltpu.make_async_copy(embed_hbm, emb_in, load_sem.at[0]),
        pltpu.make_async_copy(table_hbm, tab, load_sem.at[1]),
        pltpu.make_async_copy(hidden_hbm, hid, load_sem.at[2]),
    ]
    for load in loads:
        load.start()

    two = 2 - 4 * core
    near = (two, 1, -1)
    far = (4, 3, 5, 2, 6, 1, 7)
    group = [(dy, dc) for dy in (2, 1, 3, 0) for dc in range(NC) if (dy, dc) != (0, 0)]
    senders = [at(dy=dy, dc=dc) for dy, dc in group]
    senders += [at(dx=dx) for dx in (2, 1, 3)]
    senders += [at(dz=-dz) for dz in near]
    senders += [at(dz=4 * d) for d in far]
    barrier = pltpu.get_barrier_semaphore()
    for device in senders:
        pl.semaphore_signal(barrier, inc=1, device_id=device, device_id_type=MESH)

    loads[0].wait()
    row = lax.broadcasted_iota(jnp.int32, (PAIR, ROWS), 0)
    col = lax.broadcasted_iota(jnp.int32, (PAIR, ROWS), 1)
    upper = (row == col).astype(BF16)
    lower = (row == col + ROWS).astype(BF16)
    for p in range(2):
        for s in range(QUARTER // STEP):
            left = p * 2 * QUARTER + s * STEP
            placed = nn(upper, emb_in[:, left : left + STEP]) + nn(
                lower, emb_in[:, left + QUARTER : left + QUARTER + STEP]
            )
            emb[p, slot, :, s * STEP : (s + 1) * STEP] = placed.astype(BF16)

    pl.semaphore_wait(barrier, len(senders))

    emb_copies = []
    for p in range(2):
        for dy in (2, 1, 3):
            copy = remote(
                emb.at[p, slot], emb.at[p, slot], emb_s.at[p, dy - 1], emb_r.at[p, dy - 1], at(dy=dy)
            )
            copy.start()
            emb_copies.append(copy)

    loads[1].wait()
    loads[2].wait()
    squashed = jnp.tanh(nt(tab[...], hid[...]) / SOFTCAP)
    capped = SOFTCAP * squashed
    exponent = jnp.exp(capped)
    entry = lax.broadcasted_iota(jnp.int32, (ENT, TOK), 0) + vocab * ENT
    hit = entry == targets_ref[...]

    lane = lax.broadcasted_iota(jnp.int32, (1, 8 * PAIR), 1)
    place = lane - slot * PAIR
    ids_row = jnp.zeros((1, 8 * PAIR), F32)
    for r in range(ROWS):
        ids_row = jnp.where((place == r) | (place == r + ROWS), ids_ref[r].astype(F32), ids_row)
    stats[slot] = jnp.zeros((8, 8 * PAIR), F32)
    stats[slot, 0:1, 0:TOK] = jnp.sum(exponent, axis=0, keepdims=True)
    stats[slot, 1:2, 0:TOK] = jnp.sum(jnp.where(hit, capped, 0.0), axis=0, keepdims=True)
    stats[slot, 2:3, :] = ids_row
    st_copies = []
    for i, (dy, dc) in enumerate(group):
        copy = remote(stats.at[slot], stats.at[slot], st_s.at[i], st_r.at[i], at(dy=dy, dc=dc))
        copy.start()
        st_copies.append(copy)
    for copy in st_copies:
        copy.wait_recv()
    total = stats[0]
    for i in range(1, 8):
        total = total + stats[i]
    normalizer = total[0:1, 0:TOK]
    picked = total[1:2, 0:TOK]
    ids_all = total[2:3, :]
    loss_ref[...] = jnp.log(normalizer) - picked
    dlogit = (
        weight_ref[...] * (exponent / normalizer - hit.astype(F32)) * (1.0 - squashed * squashed)
    ).astype(BF16)

    def named(shape):
        i = lax.broadcasted_iota(jnp.int32, shape, 0)
        third, inner = i // 32, lax.rem(i, 32)
        cls, k = inner // 8, lax.rem(inner, 8)
        return 3 * (4 * k + cls) + third

    order = (named((ENT, ENT)) == lax.broadcasted_iota(jnp.int32, (ENT, ENT), 1)).astype(BF16)
    ordered = nn(order, dlogit).astype(BF16)
    named_id = (named((ENT, 8 * PAIR)) + vocab * ENT).astype(F32)
    is_lower = lax.rem(lax.broadcasted_iota(jnp.int32, (ENT, 8 * PAIR), 1), PAIR) >= ROWS
    match = named_id == ids_all
    wanted = [
        (match & jnp.logical_not(is_lower)).astype(BF16),
        (match & is_lower).astype(BF16),
    ]

    def forward(p):
        mine = emb.at[p, pl.ds(core * NY, NY)]
        return remote(mine, mine, fwd_s.at[p], fwd_r.at[p], at(dc=1))

    scale = math.sqrt(D)
    x_copy = lambda to, j: remote(
        xs.at[to, j],
        xr.at[lax.rem(x - to + NX, NX) - 1, j],
        x_s.at[to, j],
        x_r.at[lax.rem(x - to + NX, NX) - 1, j],
        (z * NX + to, vocab),
    )
    fwd_copies = []
    for p in range(2):
        for copy in emb_copies[3 * p : 3 * p + 3]:
            copy.wait_recv()
        copy = forward(p)
        copy.start()
        fwd_copies.append(copy)
        copy.wait_recv()
        for h in range(2):
            q = 2 * p + h
            for s in range(QUARTER // STEP):
                cols = slice(s * STEP, (s + 1) * STEP)
                rows = emb[p, :, :, cols].reshape(8 * PAIR, STEP)
                part = nn(ordered, hid[:, q * QUARTER + s * STEP : q * QUARTER + (s + 1) * STEP])
                part = part + scale * nn(wanted[h], rows)
                for r in range(3):
                    to, j = divmod(4 * r + q, 3)
                    mine = part[32 * r : 32 * (r + 1)]
                    xs[to, j, :, cols] = mine.astype(BF16)

                    @pl.when(x == to)
                    def _(mine=mine, j=j, cols=cols):
                        xown[j, :, cols] = mine

            for r in range(3):
                to, j = divmod(4 * r + q, 3)

                @pl.when(x != to)
                def _(to=to, j=j):
                    x_copy(to, j).start()

    for p in range(2):
        for s in range(QUARTER // STEP):
            left = p * 2 * QUARTER + s * STEP
            a = tn(dlogit, tab[:, left : left + STEP])
            b = tn(dlogit, tab[:, left + QUARTER : left + QUARTER + STEP])
            for v in range(8):
                take = slice(ROWS * v, ROWS * (v + 1))
                acc[p, v, :, s * STEP : (s + 1) * STEP] = jnp.concatenate([a[take], b[take]], axis=0)
    core_copies = []
    for p in range(2):
        for to in range(NY):
            ig_core[p, to] = acc[p, 2 * to + 1 - core].astype(BF16)
        copy = remote(ig_core.at[p], ig_core_in.at[p], c_s.at[p], c_r.at[p], at(dc=1))
        copy.start()
        core_copies.append(copy)

    for j in range(3):
        for d in range(3):
            remote(xs.at[0, j], xr.at[d, j], x_s.at[0, j], x_r.at[d, j], at(dx=1)).wait_recv()
        units[j] = (
            xown[j] + xr[0, j].astype(F32) + xr[1, j].astype(F32) + xr[2, j].astype(F32)
        )
    for c in range(4):
        rows = slice(8 * c, 8 * (c + 1))
        zf[c, 0:8, 0:1152] = units[0, rows, :]
        zf[c, 0:8, 1152:1792] = units[1, rows, 0:640]
        zf[c, 8:16, 0:512] = units[1, rows, 640:1152]
        zf[c, 8:16, 512:1664] = units[2, rows, :]
        zf[c, 8:16, 1664:1792] = jnp.zeros((8, 128), F32)
        zs[c] = zf[c].astype(BF16)
    z1_copies = []
    for i, dz in enumerate(near):
        copy = remote(
            zs.at[lax.rem(z + dz + 4, 4)], zr1.at[i], z1_s.at[i], z1_r.at[i], at(dz=dz)
        )
        copy.start()
        z1_copies.append(copy)

    y_copies = []
    for p in range(2):
        core_copies[p].wait_recv()
        for dy in (2, 1, 3, 0):
            to = lax.rem(y + dy, NY)
            both = acc[p, 2 * to + core] + ig_core_in[p, to].astype(F32)
            if dy == 0:
                ig_own[p] = both
            else:
                ig_y[p, dy - 1] = both.astype(BF16)
                copy = remote(
                    ig_y.at[p, dy - 1], ig_y_in.at[p, dy - 1], y_s.at[p, dy - 1], y_r.at[p, dy - 1], at(dy=dy)
                )
                copy.start()
                y_copies.append(copy)

    for copy in z1_copies:
        copy.wait_recv()
    part = (
        zf[lax.rem(z, 4)] + zr1[0].astype(F32) + zr1[1].astype(F32) + zr1[2].astype(F32)
    )
    zb[...] = jnp.zeros_like(zb)
    for line in range(27):
        up, at_line = divmod(line, 14)
        zb[:, line, :] = part[8 * up : 8 * (up + 1), 128 * at_line : 128 * (at_line + 1)]
    zm[...] = zb[...].astype(BF16)
    z2_copies = []
    for d in far:
        copy = remote(
            zm.at[lax.rem(z // 4 + d, 8)], zr2.at[d - 1], z2_s.at[d - 1], z2_r.at[d - 1], at(dz=4 * d)
        )
        copy.start()
        z2_copies.append(copy)

    for copy in y_copies:
        copy.wait_recv()
    for p in range(2):
        whole = ig_own[p]
        for i in range(3):
            whole = whole + ig_y_in[p, i].astype(F32)
        input_ref[:, p * 2 * QUARTER : p * 2 * QUARTER + QUARTER] = whole[:ROWS].astype(BF16)
        input_ref[:, p * 2 * QUARTER + QUARTER : (p + 1) * 2 * QUARTER] = whole[ROWS:].astype(BF16)

    for copy in emb_copies + fwd_copies + st_copies + core_copies + y_copies + z1_copies:
        copy.wait_send()
    for to in range(NX):
        for j in range(3):

            @pl.when(x != to)
            def _(to=to, j=j):
                x_copy(to, j).wait_send()

    for copy in z2_copies:
        copy.wait_recv()
    lines = zb[z // 4]
    for i in range(7):
        lines = lines + zr2[i].astype(F32)
    table_grad_ref[...] = lines[:27].astype(BF16)
    for copy in z2_copies:
        copy.wait_send()


def body(hidden, table, targets, loss_weight, token_ids, grad_embed):
    vmem = pl.BlockSpec(memory_space=pltpu.VMEM)
    hbm = pl.BlockSpec(memory_space=pl.ANY)
    sem = pltpu.SemaphoreType.DMA
    token_loss, input_grad, table_grad = pl.pallas_call(
        kernel,
        out_shape=(
            jax.ShapeDtypeStruct((1, TOK), F32),
            jax.ShapeDtypeStruct((ROWS, D), BF16),
            jax.ShapeDtypeStruct((27, 128), BF16),
        ),
        in_specs=[hbm, hbm, hbm, vmem, vmem, pl.BlockSpec(memory_space=pltpu.SMEM)],
        out_specs=(vmem, vmem, vmem),
        scratch_shapes=[
            pltpu.VMEM((TOK, D), BF16),
            pltpu.VMEM((ENT, D), BF16),
            pltpu.VMEM((ROWS, D), BF16),
            pltpu.VMEM((2, 8, PAIR, QUARTER), BF16),
            pltpu.VMEM((8, 8, 8 * PAIR), F32),
            pltpu.VMEM((NX, 3, 32, QUARTER), BF16),
            pltpu.VMEM((3, 32, QUARTER), F32),
            pltpu.VMEM((3, 3, 32, QUARTER), BF16),
            pltpu.VMEM((2, 8, PAIR, QUARTER), F32),
            pltpu.VMEM((2, NY, PAIR, QUARTER), BF16),
            pltpu.VMEM((2, NY, PAIR, QUARTER), BF16),
            pltpu.VMEM((2, PAIR, QUARTER), F32),
            pltpu.VMEM((2, 3, PAIR, QUARTER), BF16),
            pltpu.VMEM((2, 3, PAIR, QUARTER), BF16),
            pltpu.VMEM((3, 32, QUARTER), F32),
            pltpu.VMEM((4, 16, HALF), F32),
            pltpu.VMEM((4, 16, HALF), BF16),
            pltpu.VMEM((3, 16, HALF), BF16),
            pltpu.VMEM((8, 32, 128), F32),
            pltpu.VMEM((8, 32, 128), BF16),
            pltpu.VMEM((7, 32, 128), BF16),
            sem((3,)),
            sem((2, 3)), sem((2, 3)),
            sem((2,)), sem((2,)),
            sem((7,)), sem((7,)),
            sem((NX, 3)), sem((3, 3)),
            sem((2,)), sem((2,)),
            sem((2, 3)), sem((2, 3)),
            sem((3,)), sem((3,)),
            sem((7,)), sem((7,)),
        ],
        compiler_params=pltpu.CompilerParams(
            collective_id=0, has_side_effects=True, vmem_limit_bytes=40 * 1024 * 1024
        ),
    )(hidden, table, grad_embed, targets.reshape(1, TOK), loss_weight.reshape(1, TOK), token_ids)
    return (token_loss.reshape(TOK), input_grad, table_grad[None])


def solution(mesh):
    return jax.shard_map(
        body,
        mesh=mesh,
        in_specs=(
            P("dp", None),
            P("vocab", None),
            P("dp"),
            P("dp"),
            P(("dp", "vocab")),
            P(("dp", "vocab"), None),
        ),
        out_specs=(P("dp"), P(("dp", "vocab"), None), P("vocab", "dp", None)),
        check_vma=False,
    )
```

time: 657 us -> 83 us (0.13); the launches traced: 648 us -> 82.8 us
  blocking collectives: 593 us -> 0 us
  Pallas kernels: 0 us -> 74.7 us
  waiting for transfers between devices: 17.5 us -> 0 us
  between operations: 14.2 us -> 0.65 us
  matrix products: 9 us -> 0 us
  starting transfers between devices: 6.91 us -> 0 us
    psum x2 -> x0, blocking collectives: 593 us -> none  [the longest x1 579 us: body(): summed_all = lax.psum(table_term, 'dp')]
    pallas_call x0 -> x1, Pallas kernels: none -> 74.7 us  [body(): pl.pallas_call(kernel, out_shape=(jax.ShapeDtypeStruct((1, TOK), F32), ja...]
    all_to_all x2 -> x0, waiting for transfers between devices: 17.5 us -> none  [the longest x1 13.9 us: body(): lax.all_to_all(outgoing, 'vocab', split_axis=0, concat_axis=0, tiled=True)]
    dot_general x5 -> x0, matrix products: 9 us -> none  [the longest x1 2.16 us: body(): embed_part = jnp.dot(wanted, arrived, preferred_element_type=jnp.float32)]
    all_to_all x2 -> x0, starting transfers between devices: 6.87 us -> none  [the longest x1 3.56 us: body(): lax.all_to_all(outgoing, 'vocab', split_axis=0, concat_axis=0, tiled=True)]
    unnamed x10 -> x15, local copies, waits for them, and re-layouts: 0.6 us -> 7.43 us
  transfers between devices with their start and end apart: 3 -> 0, of which waited for: 2 -> 0; matrix products, arithmetic and copies ran while one was open for 2% -> 0% of each run, Pallas kernels for 0% -> 0%
where the time goes in v1:
time: 83 us; the launch traced here: 82.8 us
  Pallas kernels  74.7 us (90%)
  local copies, waits for them, and re-layouts  7.43 us (9%)
    pallas_call x1, Pallas kernels, body(): pl.pallas_call(kernel, out_shape=(jax.ShapeDtypeStruct((1, TOK), F32), ja...  74.7 us
    unnamed x15, local copies, waits for them, and re-layouts  7.43 us

profile of v1, /device:TPU:6, one launch (start us, length us, event | category | flops | bytes accessed | tf_op | source)
XLA Modules:
  0.0 82.8 jit_solution(8666762527331639832)
XLA Ops:
  0.6 0.0 copy-start
  0.6 1.5 %copy-done = bf16[192,4608]{1,0:T(8,128)(2,1)S(1)} copy-done((bf16[192,4608]{1,0:T(8,128)(2,1)S(1)}, bf16[192,4608]{1,0:T(8,128)(2,1)}, u32[]{:S(2)}) %copy-start) | copy-done | bytes 1769496
  2.1 0.0 copy-start.1
  2.1 1.2 %copy-done.1 = bf16[96,4608]{1,0:T(8,128)(2,1)S(1)} copy-done((bf16[96,4608]{1,0:T(8,128)(2,1)S(1)}, bf16[96,4608]{1,0:T(8,128)(2,1)}, u32[]{:S(2)}) %copy-start.1) | copy-done | bytes 884760
  3.3 0.0 copy-start.2
  3.3 0.9 %copy-done.2 = bf16[24,4608]{1,0:T(8,128)(2,1)S(1)} copy-done((bf16[24,4608]{1,0:T(8,128)(2,1)S(1)}, bf16[24,4608]{1,0:T(8,128)(2,1)}, u32[]{:S(2)}) %copy-start.2) | copy-done | bytes 221208
  4.2 0.0 copy-start.3
  4.2 0.7 copy-done.3
  4.9 0.0 copy-start.4
  4.9 0.7 copy-done.4
  5.6 0.0 copy-start.5
  5.6 0.7 copy-done.5
  6.2 74.7 %shard_map.85 = (f32[1,192]{1,0:T(1,128)S(1)}, bf16[24,4608]{1,0:T(8,128)(2,1)S(1)}, bf16[27,128]{1,0:T(8,128)(2,1)S(1)}) custom-call(bf16[192,4608]{1,0:T(8,128)(2,1)S(1)} %copy-done, bf16[96,4608]{1,0:T(8,128)(2,1)S(1)} %copy-done.1, bf16[24,4608]{1,0:T(8,128)(2,1)S(1)} %copy-done.2, s32[1,192]{1,0:T(1,128)S(1)} %bitcast.5, f32[1,192]{1,0:T(1,128)S(1)} %bitcast.6, ...), custom_call_target="tpu_custom_call" | custom-call | tf_op jit(solution)/shard_map/pallas_call | solution.py:304
  80.9 0.6 copy.12
  81.5 0.7 copy.13
  82.2 0.6 copy.14
Async XLA Ops:
  0.6 1.5 %copy-start = (bf16[192,4608]{1,0:T(8,128)(2,1)S(1)}, bf16[192,4608]{1,0:T(8,128)(2,1)}, u32[]{:S(2)}) copy-start(bf16[192,4608]{1,0:T(8,128)(2,1)} %hidden_hbm.1) | copy-start | bytes 5308420
  2.1 1.2 %copy-start.1 = (bf16[96,4608]{1,0:T(8,128)(2,1)S(1)}, bf16[96,4608]{1,0:T(8,128)(2,1)}, u32[]{:S(2)}) copy-start(bf16[96,4608]{1,0:T(8,128)(2,1)} %table_hbm.1) | copy-start | bytes 2654212
  3.3 0.9 %copy-start.2 = (bf16[24,4608]{1,0:T(8,128)(2,1)S(1)}, bf16[24,4608]{1,0:T(8,128)(2,1)}, u32[]{:S(2)}) copy-start(bf16[24,4608]{1,0:T(8,128)(2,1)} %embed_hbm.1) | copy-start | bytes 663556
  4.2 0.7 copy-start.3
  4.9 0.7 copy-start.4
  5.6 0.7 copy-start.5

commit v2 on v1

--- a/solution.py
+++ b/solution.py
@@ -37,11 +37,11 @@
 
 
 def kernel(
-    hidden_hbm, table_hbm, embed_hbm, targets_ref, weight_ref, ids_ref,
+    hidden_hbm, table_hbm, embed_hbm, targets_hbm, weight_hbm, ids_hbm,
     loss_ref, input_ref, table_grad_ref,
-    hid, tab, emb_in, emb, stats, xs, xown, xr, acc, ig_core, ig_core_in, ig_own, ig_y, ig_y_in,
+    hid, tab, emb_in, targets_ref, weight_ref, ids_ref, emb, stats, xs, xown, xr, acc, ig_core, ig_core_in, ig_own, ig_y, ig_y_in,
     units, zf, zs, zr1, zb, zm, zr2,
-    load_sem, emb_s, emb_r, fwd_s, fwd_r, st_s, st_r, x_s, x_r, c_s, c_r, y_s, y_r, z1_s, z1_r, z2_s, z2_r,
+    load_sem, in2_sem, in4_sem, in8_sem, emb_s, emb_r, fwd_s, fwd_r, st_s, st_r, x_s, x_r, c_s, c_r, y_s, y_r, z1_s, z1_r, z2_s, z2_r,
 ):
     dp = lax.axis_index("dp")
     vocab = lax.axis_index("vocab")
@@ -63,6 +63,9 @@
         pltpu.make_async_copy(embed_hbm, emb_in, load_sem.at[0]),
         pltpu.make_async_copy(table_hbm, tab, load_sem.at[1]),
         pltpu.make_async_copy(hidden_hbm, hid, load_sem.at[2]),
+        pltpu.make_async_copy(targets_hbm, targets_ref, load_sem.at[3]),
+        pltpu.make_async_copy(weight_hbm, weight_ref, load_sem.at[4]),
+        pltpu.make_async_copy(ids_hbm, ids_ref, load_sem.at[5]),
     ]
     for load in loads:
         load.start()
@@ -71,12 +74,11 @@
     near = (two, 1, -1)
     far = (4, 3, 5, 2, 6, 1, 7)
     group = [(dy, dc) for dy in (2, 1, 3, 0) for dc in range(NC) if (dy, dc) != (0, 0)]
-    senders = [at(dy=dy, dc=dc) for dy, dc in group]
-    senders += [at(dx=dx) for dx in (2, 1, 3)]
-    senders += [at(dz=-dz) for dz in near]
-    senders += [at(dz=4 * d) for d in far]
+    greeted = [at(dy=dy, dc=dc) for dy, dc in group]
+    greeted += [at(dx=dx) for dx in (2, 1, 3)]
+    greeted += [at(dz=dz) for dz in (1, -1, 2, -2)]
     barrier = pltpu.get_barrier_semaphore()
-    for device in senders:
+    for device in greeted:
         pl.semaphore_signal(barrier, inc=1, device_id=device, device_id_type=MESH)
 
     loads[0].wait()
@@ -92,10 +94,15 @@
             )
             emb[p, slot, :, s * STEP : (s + 1) * STEP] = placed.astype(BF16)
 
-    pl.semaphore_wait(barrier, len(senders))
+    pl.semaphore_wait(barrier, len(greeted))
+
+    def pass_on(reach, heard):
+        for dz in (reach, -reach):
+            pl.semaphore_signal(heard, inc=1, device_id=at(dz=dz), device_id_type=MESH)
 
     emb_copies = []
-    for p in range(2):
+
+    def send_rows(p):
         for dy in (2, 1, 3):
             copy = remote(
                 emb.at[p, slot], emb.at[p, slot], emb_s.at[p, dy - 1], emb_r.at[p, dy - 1], at(dy=dy)
@@ -103,8 +110,12 @@
             copy.start()
             emb_copies.append(copy)
 
+    send_rows(0)
+    pass_on(2, in2_sem)
+
     loads[1].wait()
-    loads[2].wait()
+    for load in loads[2:]:
+        load.wait()
     squashed = jnp.tanh(nt(tab[...], hid[...]) / SOFTCAP)
     capped = SOFTCAP * squashed
     exponent = jnp.exp(capped)
@@ -125,6 +136,7 @@
         copy = remote(stats.at[slot], stats.at[slot], st_s.at[i], st_r.at[i], at(dy=dy, dc=dc))
         copy.start()
         st_copies.append(copy)
+    send_rows(1)
     for copy in st_copies:
         copy.wait_recv()
     total = stats[0]
@@ -137,6 +149,9 @@
     dlogit = (
         weight_ref[...] * (exponent / normalizer - hit.astype(F32)) * (1.0 - squashed * squashed)
     ).astype(BF16)
+
+    pl.semaphore_wait(in2_sem, 2)
+    pass_on(4, in4_sem)
 
     def named(shape):
         i = lax.broadcasted_iota(jnp.int32, shape, 0)
@@ -212,6 +227,9 @@
         copy = remote(ig_core.at[p], ig_core_in.at[p], c_s.at[p], c_r.at[p], at(dc=1))
         copy.start()
         core_copies.append(copy)
+
+    pl.semaphore_wait(in4_sem, 2)
+    pass_on(8, in8_sem)
 
     for j in range(3):
         for d in range(3):
@@ -261,6 +279,7 @@
         up, at_line = divmod(line, 14)
         zb[:, line, :] = part[8 * up : 8 * (up + 1), 128 * at_line : 128 * (at_line + 1)]
     zm[...] = zb[...].astype(BF16)
+    pl.semaphore_wait(in8_sem, 2)
     z2_copies = []
     for d in far:
         copy = remote(
@@ -308,12 +327,15 @@
             jax.ShapeDtypeStruct((ROWS, D), BF16),
             jax.ShapeDtypeStruct((27, 128), BF16),
         ),
-        in_specs=[hbm, hbm, hbm, vmem, vmem, pl.BlockSpec(memory_space=pltpu.SMEM)],
+        in_specs=[hbm] * 6,
         out_specs=(vmem, vmem, vmem),
         scratch_shapes=[
             pltpu.VMEM((TOK, D), BF16),
             pltpu.VMEM((ENT, D), BF16),
             pltpu.VMEM((ROWS, D), BF16),
+            pltpu.VMEM((1, TOK), jnp.int32),
+            pltpu.VMEM((1, TOK), F32),
+            pltpu.SMEM((ROWS,), jnp.int32),
             pltpu.VMEM((2, 8, PAIR, QUARTER), BF16),
             pltpu.VMEM((8, 8, 8 * PAIR), F32),
             pltpu.VMEM((NX, 3, 32, QUARTER), BF16),
@@ -332,7 +354,8 @@
             pltpu.VMEM((8, 32, 128), F32),
             pltpu.VMEM((8, 32, 128), BF16),
             pltpu.VMEM((7, 32, 128), BF16),
-            sem((3,)),
+            sem((6,)),
+            pltpu.SemaphoreType.REGULAR, pltpu.SemaphoreType.REGULAR, pltpu.SemaphoreType.REGULAR,
             sem((2, 3)), sem((2, 3)),
             sem((2,)), sem((2,)),
             sem((7,)), sem((7,)),
@@ -343,7 +366,7 @@
             sem((7,)), sem((7,)),
         ],
         compiler_params=pltpu.CompilerParams(
-            collective_id=0, has_side_effects=True, vmem_limit_bytes=40 * 1024 * 1024
+            collective_id=0, has_side_effects=True, vmem_limit_bytes=56 * 1024 * 1024
         ),
     )(hidden, table, grad_embed, targets.reshape(1, TOK), loss_weight.reshape(1, TOK), token_ids)
     return (token_loss.reshape(TOK), input_grad, table_grad[None])

time: 83 us -> 72.2 us (0.87)
  the two profiles are of different devices: /device:TPU:6 before, /device:TPU:2 now
where the time goes in v2:
time: 72.2 us; the launch traced here: 71.9 us
  Pallas kernels  67.1 us (93%)
  local copies, waits for them, and re-layouts  4.16 us (6%)
    pallas_call x1, Pallas kernels, body(): pl.pallas_call(kernel, out_shape=(jax.ShapeDtypeStruct((1, TOK), F32), ja...  67.1 us
    unnamed x3, local copies, waits for them, and re-layouts  4.16 us

profile of v2, /device:TPU:2, one launch (start us, length us, event | category | flops | bytes accessed | tf_op | source)
XLA Modules:
  0.0 71.9 jit_solution(16584606680769277760)
XLA Ops:
  0.6 67.1 %shard_map.85 = (f32[1,192]{1,0:T(1,128)}, bf16[24,4608]{1,0:T(8,128)(2,1)}, bf16[27,128]{1,0:T(8,128)(2,1)}) custom-call(bf16[192,4608]{1,0:T(8,128)(2,1)} %hidden_hbm.1, bf16[96,4608]{1,0:T(8,128)(2,1)} %table_hbm.1, bf16[24,4608]{1,0:T(8,128)(2,1)} %embed_hbm.1, s32[1,192]{1,0:T(1,128)} %bitcast.5, f32[1,192]{1,0:T(1,128)} %bitcast.6, s32[24]{0:T(128)} %ids_hbm.1), custom_call_target="tpu_custom_call" | custom-call | tf_op jit(solution)/shard_map/pallas_call | solution.py:323
  67.8 1.2 %copy.12 = f32[192]{0:T(256)} copy(f32[192]{0:T(256)} %bitcast.7) | data formatting | bytes 1536
  69.0 1.6 %copy.13 = bf16[24,4608]{1,0:T(8,128)(2,1)} copy(bf16[24,4608]{1,0:T(8,128)(2,1)} %get-tuple-element.13) | data formatting | bytes 442368
  70.6 1.3 %copy.14 = bf16[1,27,128]{2,1,0:T(8,128)(2,1)} copy(bf16[1,27,128]{2,1,0:T(8,128)(2,1)} %bitcast.4) | data formatting | bytes 13824

commit v3 on v2

--- a/solution.py
+++ b/solution.py
@@ -19,7 +19,9 @@
 ROWS = 24
 QUARTER = D // 4
 PAIR = 2 * ROWS
-HALF = 1792
+PART_A = 640
+PART_B = QUARTER - PART_A
+HALF = 1024
 STEP = 384
 NX, NY, NZ, NC = 4, 4, 32, 2
 
@@ -40,8 +42,8 @@
     hidden_hbm, table_hbm, embed_hbm, targets_hbm, weight_hbm, ids_hbm,
     loss_ref, input_ref, table_grad_ref,
     hid, tab, emb_in, targets_ref, weight_ref, ids_ref, emb, stats, xs, xown, xr, acc, ig_core, ig_core_in, ig_own, ig_y, ig_y_in,
-    units, zf, zs, zr1, zb, zm, zr2,
-    load_sem, in2_sem, in4_sem, in8_sem, emb_s, emb_r, fwd_s, fwd_r, st_s, st_r, x_s, x_r, c_s, c_r, y_s, y_r, z1_s, z1_r, z2_s, z2_r,
+    units, zf, zs, zr1, bf, bs, br1, b2f, b2, b2r, zb, zm, zr2,
+    load_sem, in2_sem, in4_sem, in8_sem, emb_s, emb_r, fwd_s, fwd_r, st_s, st_r, x_s, x_r, c_s, c_r, y_s, y_r, z1_s, z1_r, b1_s, b1_r, b2_s, b2_r, z2_s, z2_r,
 ):
     dp = lax.axis_index("dp")
     vocab = lax.axis_index("vocab")
@@ -137,6 +139,8 @@
         copy.start()
         st_copies.append(copy)
     send_rows(1)
+    pl.semaphore_wait(in2_sem, 2)
+    pass_on(4, in4_sem)
     for copy in st_copies:
         copy.wait_recv()
     total = stats[0]
@@ -150,9 +154,6 @@
         weight_ref[...] * (exponent / normalizer - hit.astype(F32)) * (1.0 - squashed * squashed)
     ).astype(BF16)
 
-    pl.semaphore_wait(in2_sem, 2)
-    pass_on(4, in4_sem)
-
     def named(shape):
         i = lax.broadcasted_iota(jnp.int32, shape, 0)
         third, inner = i // 32, lax.rem(i, 32)
@@ -182,6 +183,7 @@
         (z * NX + to, vocab),
     )
     fwd_copies = []
+    b1_copies = []
     for p in range(2):
         for copy in emb_copies[3 * p : 3 * p + 3]:
             copy.wait_recv()
@@ -191,19 +193,25 @@
         copy.wait_recv()
         for h in range(2):
             q = 2 * p + h
-            for s in range(QUARTER // STEP):
-                cols = slice(s * STEP, (s + 1) * STEP)
-                rows = emb[p, :, :, cols].reshape(8 * PAIR, STEP)
-                part = nn(ordered, hid[:, q * QUARTER + s * STEP : q * QUARTER + (s + 1) * STEP])
+            for lo, hi in ((0, 384), (384, PART_A), (PART_A, QUARTER)):
+                rows = emb[p, :, :, lo:hi].reshape(8 * PAIR, hi - lo)
+                part = nn(ordered, hid[:, q * QUARTER + lo : q * QUARTER + hi])
                 part = part + scale * nn(wanted[h], rows)
                 for r in range(3):
+                    if lo == PART_A:
+                        for c in range(4):
+                            eight = part[32 * r + 8 * c : 32 * r + 8 * (c + 1)]
+                            folded = jnp.concatenate([eight[:, : PART_B // 2], eight[:, PART_B // 2 :]], axis=0)
+                            bf[c, p, 2 * r + h] = folded
+                            bs[c, p, 2 * r + h] = folded.astype(BF16)
+                        continue
                     to, j = divmod(4 * r + q, 3)
                     mine = part[32 * r : 32 * (r + 1)]
-                    xs[to, j, :, cols] = mine.astype(BF16)
+                    xs[to, j, :, lo:hi] = mine.astype(BF16)
 
                     @pl.when(x == to)
-                    def _(mine=mine, j=j, cols=cols):
-                        xown[j, :, cols] = mine
+                    def _(mine=mine, j=j, lo=lo, hi=hi):
+                        xown[j, :, lo:hi] = mine
 
             for r in range(3):
                 to, j = divmod(4 * r + q, 3)
@@ -211,6 +219,16 @@
                 @pl.when(x != to)
                 def _(to=to, j=j):
                     x_copy(to, j).start()
+
+        for i, dz in enumerate(near):
+            copy = remote(
+                bs.at[lax.rem(z + dz + 4, 4), p], br1.at[i, p], b1_s.at[i, p], b1_r.at[i, p], at(dz=dz)
+            )
+            copy.start()
+            b1_copies.append(copy)
+
+    pl.semaphore_wait(in4_sem, 2)
+    pass_on(8, in8_sem)
 
     for p in range(2):
         for s in range(QUARTER // STEP):
@@ -228,9 +246,6 @@
         copy.start()
         core_copies.append(copy)
 
-    pl.semaphore_wait(in4_sem, 2)
-    pass_on(8, in8_sem)
-
     for j in range(3):
         for d in range(3):
             remote(xs.at[0, j], xr.at[d, j], x_s.at[0, j], x_r.at[d, j], at(dx=1)).wait_recv()
@@ -239,11 +254,11 @@
         )
     for c in range(4):
         rows = slice(8 * c, 8 * (c + 1))
-        zf[c, 0:8, 0:1152] = units[0, rows, :]
-        zf[c, 0:8, 1152:1792] = units[1, rows, 0:640]
-        zf[c, 8:16, 0:512] = units[1, rows, 640:1152]
-        zf[c, 8:16, 512:1664] = units[2, rows, :]
-        zf[c, 8:16, 1664:1792] = jnp.zeros((8, 128), F32)
+        zf[c, 0:8, 0:640] = units[0, rows, :]
+        zf[c, 0:8, 640:1024] = units[1, rows, 0:384]
+        zf[c, 8:16, 0:256] = units[1, rows, 384:640]
+        zf[c, 8:16, 256:896] = units[2, rows, :]
+        zf[c, 8:16, 896:1024] = jnp.zeros((8, 128), F32)
         zs[c] = zf[c].astype(BF16)
     z1_copies = []
     for i, dz in enumerate(near):
@@ -252,6 +267,23 @@
         )
         copy.start()
         z1_copies.append(copy)
+
+    for copy in b1_copies:
+        copy.wait_recv()
+    for p in range(2):
+        for i in range(6):
+            r, h = divmod(i, 2)
+            to, j = divmod(4 * r + 2 * p + h, 3)
+            four = bf[lax.rem(z, 4), p, i]
+            for n in range(3):
+                four = four + br1[n, p, i].astype(F32)
+            b2f[to, j] = four
+            b2[to, j] = four.astype(BF16)
+    b2_copies = []
+    for i, dx in enumerate((1, 2, 3)):
+        copy = remote(b2.at[lax.rem(x + dx, NX)], b2r.at[i], b2_s.at[i], b2_r.at[i], at(dx=dx))
+        copy.start()
+        b2_copies.append(copy)
 
     y_copies = []
     for p in range(2):
@@ -269,15 +301,22 @@
                 copy.start()
                 y_copies.append(copy)
 
-    for copy in z1_copies:
+    for copy in z1_copies + b2_copies:
         copy.wait_recv()
     part = (
         zf[lax.rem(z, 4)] + zr1[0].astype(F32) + zr1[1].astype(F32) + zr1[2].astype(F32)
     )
     zb[...] = jnp.zeros_like(zb)
-    for line in range(27):
-        up, at_line = divmod(line, 14)
-        zb[:, line, :] = part[8 * up : 8 * (up + 1), 128 * at_line : 128 * (at_line + 1)]
+    for j in range(3):
+        lower_part = b2f[x, j]
+        for n in range(3):
+            lower_part = lower_part + b2r[n, j].astype(F32)
+        for line in range(5):
+            up, at_line = divmod(5 * j + line, 8)
+            zb[:, 9 * j + line, :] = part[8 * up : 8 * (up + 1), 128 * at_line : 128 * (at_line + 1)]
+        for line in range(4):
+            up, at_line = divmod(line, 2)
+            zb[:, 9 * j + 5 + line, :] = lower_part[8 * up : 8 * (up + 1), 128 * at_line : 128 * (at_line + 1)]
     zm[...] = zb[...].astype(BF16)
     pl.semaphore_wait(in8_sem, 2)
     z2_copies = []
@@ -297,7 +336,7 @@
         input_ref[:, p * 2 * QUARTER : p * 2 * QUARTER + QUARTER] = whole[:ROWS].astype(BF16)
         input_ref[:, p * 2 * QUARTER + QUARTER : (p + 1) * 2 * QUARTER] = whole[ROWS:].astype(BF16)
 
-    for copy in emb_copies + fwd_copies + st_copies + core_copies + y_copies + z1_copies:
+    for copy in emb_copies + fwd_copies + st_copies + core_copies + y_copies + z1_copies + b1_copies + b2_copies:
         copy.wait_send()
     for to in range(NX):
         for j in range(3):
@@ -316,11 +355,29 @@
         copy.wait_send()
 
 
+def hand_over(a, b, c, a_out, b_out, c_out, a_mid, b_mid, c_mid, in_sem, out_sem):
+    arrive = [
+        pltpu.make_async_copy(src, mid, in_sem.at[i])
+        for i, (src, mid) in enumerate(((a, a_mid), (b, b_mid), (c, c_mid)))
+    ]
+    leave = [
+        pltpu.make_async_copy(mid, dst, out_sem.at[i])
+        for i, (mid, dst) in enumerate(((a_mid, a_out), (b_mid, b_out), (c_mid, c_out)))
+    ]
+    for copy in arrive:
+        copy.start()
+    for come, go in zip(arrive, leave):
+        come.wait()
+        go.start()
+    for copy in leave:
+        copy.wait()
+
+
 def body(hidden, table, targets, loss_weight, token_ids, grad_embed):
     vmem = pl.BlockSpec(memory_space=pltpu.VMEM)
     hbm = pl.BlockSpec(memory_space=pl.ANY)
     sem = pltpu.SemaphoreType.DMA
-    token_loss, input_grad, table_grad = pl.pallas_call(
+    results = pl.pallas_call(
         kernel,
         out_shape=(
             jax.ShapeDtypeStruct((1, TOK), F32),
@@ -338,19 +395,25 @@
             pltpu.SMEM((ROWS,), jnp.int32),
             pltpu.VMEM((2, 8, PAIR, QUARTER), BF16),
             pltpu.VMEM((8, 8, 8 * PAIR), F32),
-            pltpu.VMEM((NX, 3, 32, QUARTER), BF16),
-            pltpu.VMEM((3, 32, QUARTER), F32),
-            pltpu.VMEM((3, 3, 32, QUARTER), BF16),
+            pltpu.VMEM((NX, 3, 32, PART_A), BF16),
+            pltpu.VMEM((3, 32, PART_A), F32),
+            pltpu.VMEM((3, 3, 32, PART_A), BF16),
             pltpu.VMEM((2, 8, PAIR, QUARTER), F32),
             pltpu.VMEM((2, NY, PAIR, QUARTER), BF16),
             pltpu.VMEM((2, NY, PAIR, QUARTER), BF16),
             pltpu.VMEM((2, PAIR, QUARTER), F32),
             pltpu.VMEM((2, 3, PAIR, QUARTER), BF16),
             pltpu.VMEM((2, 3, PAIR, QUARTER), BF16),
-            pltpu.VMEM((3, 32, QUARTER), F32),
+            pltpu.VMEM((3, 32, PART_A), F32),
             pltpu.VMEM((4, 16, HALF), F32),
             pltpu.VMEM((4, 16, HALF), BF16),
             pltpu.VMEM((3, 16, HALF), BF16),
+            pltpu.VMEM((4, 2, 6, 16, PART_B // 2), F32),
+            pltpu.VMEM((4, 2, 6, 16, PART_B // 2), BF16),
+            pltpu.VMEM((3, 2, 6, 16, PART_B // 2), BF16),
+            pltpu.VMEM((NX, 3, 16, PART_B // 2), F32),
+            pltpu.VMEM((NX, 3, 16, PART_B // 2), BF16),
+            pltpu.VMEM((3, 3, 16, PART_B // 2), BF16),
             pltpu.VMEM((8, 32, 128), F32),
             pltpu.VMEM((8, 32, 128), BF16),
             pltpu.VMEM((7, 32, 128), BF16),
@@ -363,12 +426,22 @@
             sem((2,)), sem((2,)),
             sem((2, 3)), sem((2, 3)),
             sem((3,)), sem((3,)),
+            sem((3, 2)), sem((3, 2)),
+            sem((3,)), sem((3,)),
             sem((7,)), sem((7,)),
         ],
         compiler_params=pltpu.CompilerParams(
             collective_id=0, has_side_effects=True, vmem_limit_bytes=56 * 1024 * 1024
         ),
     )(hidden, table, grad_embed, targets.reshape(1, TOK), loss_weight.reshape(1, TOK), token_ids)
+    token_loss, input_grad, table_grad = pl.pallas_call(
+        hand_over,
+        out_shape=tuple(jax.ShapeDtypeStruct(r.shape, r.dtype) for r in results),
+        in_specs=[hbm] * 3,
+        out_specs=(hbm,) * 3,
+        scratch_shapes=[pltpu.VMEM(r.shape, r.dtype) for r in results] + [sem((3,)), sem((3,))],
+        compiler_params=pltpu.CompilerParams(vmem_limit_bytes=56 * 1024 * 1024),
+    )(*results)
     return (token_loss.reshape(TOK), input_grad, table_grad[None])
 
 

time: 72.2 us -> 63.7 us (0.88)
  the two profiles are of different devices: /device:TPU:2 before, /device:TPU:8 now
where the time goes in v3:
time: 63.7 us; the launch traced here: 63.5 us
  Pallas kernels  62.9 us (99%)
  between operations  0.64 us (1%)
    pallas_call x1, Pallas kernels, body(): pl.pallas_call(kernel, out_shape=(jax.ShapeDtypeStruct((1, TOK), F32), ja...  61.2 us
    pallas_call x1, Pallas kernels, body(): pl.pallas_call(hand_over, out_shape=tuple((jax.ShapeDtypeStruct(r.shape,...  1.68 us

profile of v3, /device:TPU:8, one launch (start us, length us, event | category | flops | bytes accessed | tf_op | source)
XLA Modules:
  0.0 63.5 jit_solution(10090323779504711320)
XLA Ops:
  0.6 61.2 %shard_map.85 = (f32[1,192]{1,0:T(1,128)}, bf16[24,4608]{1,0:T(8,128)(2,1)}, bf16[27,128]{1,0:T(8,128)(2,1)}) custom-call(bf16[192,4608]{1,0:T(8,128)(2,1)} %hidden_hbm.1, bf16[96,4608]{1,0:T(8,128)(2,1)} %table_hbm.1, bf16[24,4608]{1,0:T(8,128)(2,1)} %embed_hbm.1, s32[1,192]{1,0:T(1,128)} %bitcast.4, f32[1,192]{1,0:T(1,128)} %bitcast.5, s32[24]{0:T(128)} %ids_hbm.1), custom_call_target="tpu_custom_call" | custom-call | tf_op jit(solution)/shard_map/pallas_call | solution.py:380
  61.8 1.7 %shard_map.86 = (f32[1,192]{1,0:T(1,128)}, bf16[24,4608]{1,0:T(8,128)(2,1)}, bf16[27,128]{1,0:T(8,128)(2,1)}) custom-call(f32[1,192]{1,0:T(1,128)} %get-tuple-element.9.a, bf16[24,4608]{1,0:T(8,128)(2,1)} %get-tuple-element.10.b, bf16[27,128]{1,0:T(8,128)(2,1)} %get-tuple-element.11.c), custom_call_target="tpu_custom_call" | custom-call | tf_op jit(solution)/shard_map/pallas_call | solution.py:437

commit v4 on v3

--- a/solution.py
+++ b/solution.py
@@ -40,10 +40,10 @@
 
 def kernel(
     hidden_hbm, table_hbm, embed_hbm, targets_hbm, weight_hbm, ids_hbm,
-    loss_ref, input_ref, table_grad_ref,
-    hid, tab, emb_in, targets_ref, weight_ref, ids_ref, emb, stats, xs, xown, xr, acc, ig_core, ig_core_in, ig_own, ig_y, ig_y_in,
+    loss_hbm, input_hbm, table_grad_hbm,
+    hid, tab, emb_in, targets_ref, weight_ref, ids_ref, loss_ref, input_ref, table_grad_ref, emb_a, emb_b, stats, xs, xown, xr, acc, ig_core, ig_core_in, ig_own, ig_y, ig_y_in,
     units, zf, zs, zr1, bf, bs, br1, b2f, b2, b2r, zb, zm, zr2,
-    load_sem, in2_sem, in4_sem, in8_sem, emb_s, emb_r, fwd_s, fwd_r, st_s, st_r, x_s, x_r, c_s, c_r, y_s, y_r, z1_s, z1_r, b1_s, b1_r, b2_s, b2_r, z2_s, z2_r,
+    load_sem, out_sem, in2_sem, in4_sem, in8_sem, emb_s, emb_r, fwd_s, fwd_r, st_s, st_r, x_s, x_r, c_s, c_r, y_s, y_r, z1_s, z1_r, b1_s, b1_r, b2_s, b2_r, z2_s, z2_r,
 ):
     dp = lax.axis_index("dp")
     vocab = lax.axis_index("vocab")
@@ -89,12 +89,13 @@
     upper = (row == col).astype(BF16)
     lower = (row == col + ROWS).astype(BF16)
     for p in range(2):
-        for s in range(QUARTER // STEP):
-            left = p * 2 * QUARTER + s * STEP
-            placed = nn(upper, emb_in[:, left : left + STEP]) + nn(
-                lower, emb_in[:, left + QUARTER : left + QUARTER + STEP]
+        for lo, hi, dst in ((0, 384, emb_a), (384, PART_A, emb_a), (PART_A, QUARTER, emb_b)):
+            left = 2 * p * QUARTER
+            placed = nn(upper, emb_in[:, left + lo : left + hi]) + nn(
+                lower, emb_in[:, left + QUARTER + lo : left + QUARTER + hi]
             )
-            emb[p, slot, :, s * STEP : (s + 1) * STEP] = placed.astype(BF16)
+            base = 0 if dst is emb_a else PART_A
+            dst[p, slot, :, lo - base : hi - base] = placed.astype(BF16)
 
     pl.semaphore_wait(barrier, len(greeted))
 
@@ -104,10 +105,13 @@
 
     emb_copies = []
 
-    def send_rows(p):
+    pieces = ((emb_a, 0), (emb_b, 0), (emb_a, 1), (emb_b, 1))
+
+    def send_rows(n):
+        rows, p = pieces[n]
         for dy in (2, 1, 3):
             copy = remote(
-                emb.at[p, slot], emb.at[p, slot], emb_s.at[p, dy - 1], emb_r.at[p, dy - 1], at(dy=dy)
+                rows.at[p, slot], rows.at[p, slot], emb_s.at[n, dy - 1], emb_r.at[n, dy - 1], at(dy=dy)
             )
             copy.start()
             emb_copies.append(copy)
@@ -138,7 +142,8 @@
         copy = remote(stats.at[slot], stats.at[slot], st_s.at[i], st_r.at[i], at(dy=dy, dc=dc))
         copy.start()
         st_copies.append(copy)
-    send_rows(1)
+    for n in (1, 2, 3):
+        send_rows(n)
     pl.semaphore_wait(in2_sem, 2)
     pass_on(4, in4_sem)
     for copy in st_copies:
@@ -150,6 +155,8 @@
     picked = total[1:2, 0:TOK]
     ids_all = total[2:3, :]
     loss_ref[...] = jnp.log(normalizer) - picked
+    loss_out = pltpu.make_async_copy(loss_ref, loss_hbm, out_sem.at[0])
+    loss_out.start()
     dlogit = (
         weight_ref[...] * (exponent / normalizer - hit.astype(F32)) * (1.0 - squashed * squashed)
     ).astype(BF16)
@@ -170,9 +177,10 @@
         (match & is_lower).astype(BF16),
     ]
 
-    def forward(p):
-        mine = emb.at[p, pl.ds(core * NY, NY)]
-        return remote(mine, mine, fwd_s.at[p], fwd_r.at[p], at(dc=1))
+    def forward(n):
+        rows, p = pieces[n]
+        mine = rows.at[p, pl.ds(core * NY, NY)]
+        return remote(mine, mine, fwd_s.at[n], fwd_r.at[n], at(dc=1))
 
     scale = math.sqrt(D)
     x_copy = lambda to, j: remote(
@@ -184,27 +192,33 @@
     )
     fwd_copies = []
     b1_copies = []
-    for p in range(2):
-        for copy in emb_copies[3 * p : 3 * p + 3]:
+    for n, (held, p) in enumerate(pieces):
+        for copy in emb_copies[3 * n : 3 * n + 3]:
             copy.wait_recv()
-        copy = forward(p)
+        copy = forward(n)
         copy.start()
         fwd_copies.append(copy)
         copy.wait_recv()
         for h in range(2):
             q = 2 * p + h
-            for lo, hi in ((0, 384), (384, PART_A), (PART_A, QUARTER)):
-                rows = emb[p, :, :, lo:hi].reshape(8 * PAIR, hi - lo)
+
+            def product(lo, hi, base):
+                rows = held[p, :, :, lo - base : hi - base].reshape(8 * PAIR, hi - lo)
                 part = nn(ordered, hid[:, q * QUARTER + lo : q * QUARTER + hi])
-                part = part + scale * nn(wanted[h], rows)
+                return part + scale * nn(wanted[h], rows)
+
+            if held is emb_b:
+                part = product(PART_A, QUARTER, PART_A)
                 for r in range(3):
-                    if lo == PART_A:
-                        for c in range(4):
-                            eight = part[32 * r + 8 * c : 32 * r + 8 * (c + 1)]
-                            folded = jnp.concatenate([eight[:, : PART_B // 2], eight[:, PART_B // 2 :]], axis=0)
-                            bf[c, p, 2 * r + h] = folded
-                            bs[c, p, 2 * r + h] = folded.astype(BF16)
-                        continue
+                    for c in range(4):
+                        eight = part[32 * r + 8 * c : 32 * r + 8 * (c + 1)]
+                        folded = jnp.concatenate([eight[:, : PART_B // 2], eight[:, PART_B // 2 :]], axis=0)
+                        bf[c, p, 2 * r + h] = folded
+                        bs[c, p, 2 * r + h] = folded.astype(BF16)
+                continue
+            for lo, hi in ((0, 384), (384, PART_A)):
+                part = product(lo, hi, 0)
+                for r in range(3):
                     to, j = divmod(4 * r + q, 3)
                     mine = part[32 * r : 32 * (r + 1)]
                     xs[to, j, :, lo:hi] = mine.astype(BF16)
@@ -220,12 +234,13 @@
                 def _(to=to, j=j):
                     x_copy(to, j).start()
 
-        for i, dz in enumerate(near):
-            copy = remote(
-                bs.at[lax.rem(z + dz + 4, 4), p], br1.at[i, p], b1_s.at[i, p], b1_r.at[i, p], at(dz=dz)
-            )
-            copy.start()
-            b1_copies.append(copy)
+        if held is emb_b:
+            for i, dz in enumerate(near):
+                copy = remote(
+                    bs.at[lax.rem(z + dz + 4, 4), p], br1.at[i, p], b1_s.at[i, p], b1_r.at[i, p], at(dz=dz)
+                )
+                copy.start()
+                b1_copies.append(copy)
 
     pl.semaphore_wait(in4_sem, 2)
     pass_on(8, in8_sem)
@@ -335,6 +350,8 @@
             whole = whole + ig_y_in[p, i].astype(F32)
         input_ref[:, p * 2 * QUARTER : p * 2 * QUARTER + QUARTER] = whole[:ROWS].astype(BF16)
         input_ref[:, p * 2 * QUARTER + QUARTER : (p + 1) * 2 * QUARTER] = whole[ROWS:].astype(BF16)
+    input_out = pltpu.make_async_copy(input_ref, input_hbm, out_sem.at[1])
+    input_out.start()
 
     for copy in emb_copies + fwd_copies + st_copies + core_copies + y_copies + z1_copies + b1_copies + b2_copies:
         copy.wait_send()
@@ -351,8 +368,12 @@
     for i in range(7):
         lines = lines + zr2[i].astype(F32)
     table_grad_ref[...] = lines[:27].astype(BF16)
+    table_out = pltpu.make_async_copy(table_grad_ref, table_grad_hbm, out_sem.at[2])
+    table_out.start()
     for copy in z2_copies:
         copy.wait_send()
+    for copy in (loss_out, input_out, table_out):
+        copy.wait()
 
 
 def hand_over(a, b, c, a_out, b_out, c_out, a_mid, b_mid, c_mid, in_sem, out_sem):
@@ -374,7 +395,6 @@
 
 
 def body(hidden, table, targets, loss_weight, token_ids, grad_embed):
-    vmem = pl.BlockSpec(memory_space=pltpu.VMEM)
     hbm = pl.BlockSpec(memory_space=pl.ANY)
     sem = pltpu.SemaphoreType.DMA
     results = pl.pallas_call(
@@ -385,7 +405,7 @@
             jax.ShapeDtypeStruct((27, 128), BF16),
         ),
         in_specs=[hbm] * 6,
-        out_specs=(vmem, vmem, vmem),
+        out_specs=(hbm,) * 3,
         scratch_shapes=[
             pltpu.VMEM((TOK, D), BF16),
             pltpu.VMEM((ENT, D), BF16),
@@ -393,7 +413,11 @@
             pltpu.VMEM((1, TOK), jnp.int32),
             pltpu.VMEM((1, TOK), F32),
             pltpu.SMEM((ROWS,), jnp.int32),
-            pltpu.VMEM((2, 8, PAIR, QUARTER), BF16),
+            pltpu.VMEM((1, TOK), F32),
+            pltpu.VMEM((ROWS, D), BF16),
+            pltpu.VMEM((27, 128), BF16),
+            pltpu.VMEM((2, 8, PAIR, PART_A), BF16),
+            pltpu.VMEM((2, 8, PAIR, PART_B), BF16),
             pltpu.VMEM((8, 8, 8 * PAIR), F32),
             pltpu.VMEM((NX, 3, 32, PART_A), BF16),
             pltpu.VMEM((3, 32, PART_A), F32),
@@ -417,10 +441,10 @@
             pltpu.VMEM((8, 32, 128), F32),
             pltpu.VMEM((8, 32, 128), BF16),
             pltpu.VMEM((7, 32, 128), BF16),
-            sem((6,)),
+            sem((6,)), sem((3,)),
             pltpu.SemaphoreType.REGULAR, pltpu.SemaphoreType.REGULAR, pltpu.SemaphoreType.REGULAR,
-            sem((2, 3)), sem((2, 3)),
-            sem((2,)), sem((2,)),
+            sem((4, 3)), sem((4, 3)),
+            sem((4,)), sem((4,)),
             sem((7,)), sem((7,)),
             sem((NX, 3)), sem((3, 3)),
             sem((2,)), sem((2,)),

time: 63.7 us -> 61.5 us (0.965)
  the two profiles are of different devices: /device:TPU:8 before, /device:TPU:6 now
where the time goes in v4:
time: 61.5 us; the launch traced here: 60.8 us
  Pallas kernels  60.2 us (98%)
  between operations  0.64 us (1%)
    pallas_call x1, Pallas kernels, body(): pl.pallas_call(kernel, out_shape=(jax.ShapeDtypeStruct((1, TOK), F32), ja...  58.5 us
    pallas_call x1, Pallas kernels, body(): pl.pallas_call(hand_over, out_shape=tuple((jax.ShapeDtypeStruct(r.shape,...  1.68 us

profile of v4, /device:TPU:6, one launch (start us, length us, event | category | flops | bytes accessed | tf_op | source)
XLA Modules:
  0.0 60.8 jit_solution(17045588944599029710)
XLA Ops:
  0.6 58.5 %shard_map.85 = (f32[1,192]{1,0:T(1,128)}, bf16[24,4608]{1,0:T(8,128)(2,1)}, bf16[27,128]{1,0:T(8,128)(2,1)}) custom-call(bf16[192,4608]{1,0:T(8,128)(2,1)} %hidden_hbm.1, bf16[96,4608]{1,0:T(8,128)(2,1)} %table_hbm.1, bf16[24,4608]{1,0:T(8,128)(2,1)} %embed_hbm.1, s32[1,192]{1,0:T(1,128)} %bitcast.4, f32[1,192]{1,0:T(1,128)} %bitcast.5, s32[24]{0:T(128)} %ids_hbm.1), custom_call_target="tpu_custom_call" | custom-call | tf_op jit(solution)/shard_map/pallas_call | solution.py:400
  59.1 1.7 %shard_map.86 = (f32[1,192]{1,0:T(1,128)}, bf16[24,4608]{1,0:T(8,128)(2,1)}, bf16[27,128]{1,0:T(8,128)(2,1)}) custom-call(f32[1,192]{1,0:T(1,128)} %get-tuple-element.9.a, bf16[24,4608]{1,0:T(8,128)(2,1)} %get-tuple-element.10.b, bf16[27,128]{1,0:T(8,128)(2,1)} %get-tuple-element.11.c), custom_call_target="tpu_custom_call" | custom-call | tf_op jit(solution)/shard_map/pallas_call | solution.py:461

commit v5 on v4

--- a/solution.py
+++ b/solution.py
@@ -133,10 +133,10 @@
     ids_row = jnp.zeros((1, 8 * PAIR), F32)
     for r in range(ROWS):
         ids_row = jnp.where((place == r) | (place == r + ROWS), ids_ref[r].astype(F32), ids_row)
-    stats[slot] = jnp.zeros((8, 8 * PAIR), F32)
-    stats[slot, 0:1, 0:TOK] = jnp.sum(exponent, axis=0, keepdims=True)
-    stats[slot, 1:2, 0:TOK] = jnp.sum(jnp.where(hit, capped, 0.0), axis=0, keepdims=True)
-    stats[slot, 2:3, :] = ids_row
+    stats[slot] = jnp.zeros((1, 896), F32)
+    stats[slot, :, 0:TOK] = jnp.sum(exponent, axis=0, keepdims=True)
+    stats[slot, :, 256 : 256 + TOK] = jnp.sum(jnp.where(hit, capped, 0.0), axis=0, keepdims=True)
+    stats[slot, :, 512:896] = ids_row
     st_copies = []
     for i, (dy, dc) in enumerate(group):
         copy = remote(stats.at[slot], stats.at[slot], st_s.at[i], st_r.at[i], at(dy=dy, dc=dc))
@@ -151,9 +151,9 @@
     total = stats[0]
     for i in range(1, 8):
         total = total + stats[i]
-    normalizer = total[0:1, 0:TOK]
-    picked = total[1:2, 0:TOK]
-    ids_all = total[2:3, :]
+    normalizer = total[:, 0:TOK]
+    picked = total[:, 256 : 256 + TOK]
+    ids_all = total[:, 512:896]
     loss_ref[...] = jnp.log(normalizer) - picked
     loss_out = pltpu.make_async_copy(loss_ref, loss_hbm, out_sem.at[0])
     loss_out.start()
@@ -295,7 +295,7 @@
             b2f[to, j] = four
             b2[to, j] = four.astype(BF16)
     b2_copies = []
-    for i, dx in enumerate((1, 2, 3)):
+    for i, dx in enumerate((2, 1, 3)):
         copy = remote(b2.at[lax.rem(x + dx, NX)], b2r.at[i], b2_s.at[i], b2_r.at[i], at(dx=dx))
         copy.start()
         b2_copies.append(copy)
@@ -418,7 +418,7 @@
             pltpu.VMEM((27, 128), BF16),
             pltpu.VMEM((2, 8, PAIR, PART_A), BF16),
             pltpu.VMEM((2, 8, PAIR, PART_B), BF16),
-            pltpu.VMEM((8, 8, 8 * PAIR), F32),
+            pltpu.VMEM((8, 1, 896), F32),
             pltpu.VMEM((NX, 3, 32, PART_A), BF16),
             pltpu.VMEM((3, 32, PART_A), F32),
             pltpu.VMEM((3, 3, 32, PART_A), BF16),

time: 61.5 us -> 61.2 us (level)
  Pallas kernels: 60.2 us -> 59.5 us
    pallas_call x1, Pallas kernels: 58.5 us -> 57.8 us  [body(): pl.pallas_call(kernel, out_shape=(jax.ShapeDtypeStruct((1, TOK), F32), ja...]
where the time goes in v5:
time: 61.2 us; the launch traced here: 60.2 us
  Pallas kernels  59.5 us (97%)
  between operations  0.64 us (1%)
    pallas_call x1, Pallas kernels, body(): pl.pallas_call(kernel, out_shape=(jax.ShapeDtypeStruct((1, TOK), F32), ja...  57.8 us
    pallas_call x1, Pallas kernels, body(): pl.pallas_call(hand_over, out_shape=tuple((jax.ShapeDtypeStruct(r.shape,...  1.68 us

profile of v5, /device:TPU:6, one launch (start us, length us, event | category | flops | bytes accessed | tf_op | source)
XLA Modules:
  0.0 60.2 jit_solution(10184209709518264196)
XLA Ops:
  0.6 57.8 %shard_map.85 = (f32[1,192]{1,0:T(1,128)}, bf16[24,4608]{1,0:T(8,128)(2,1)}, bf16[27,128]{1,0:T(8,128)(2,1)}) custom-call(bf16[192,4608]{1,0:T(8,128)(2,1)} %hidden_hbm.1, bf16[96,4608]{1,0:T(8,128)(2,1)} %table_hbm.1, bf16[24,4608]{1,0:T(8,128)(2,1)} %embed_hbm.1, s32[1,192]{1,0:T(1,128)} %bitcast.4, f32[1,192]{1,0:T(1,128)} %bitcast.5, s32[24]{0:T(128)} %ids_hbm.1), custom_call_target="tpu_custom_call" | custom-call | tf_op jit(solution)/shard_map/pallas_call | solution.py:400
  58.5 1.7 %shard_map.86 = (f32[1,192]{1,0:T(1,128)}, bf16[24,4608]{1,0:T(8,128)(2,1)}, bf16[27,128]{1,0:T(8,128)(2,1)}) custom-call(f32[1,192]{1,0:T(1,128)} %get-tuple-element.9.a, bf16[24,4608]{1,0:T(8,128)(2,1)} %get-tuple-element.10.b, bf16[27,128]{1,0:T(8,128)(2,1)} %get-tuple-element.11.c), custom_call_target="tpu_custom_call" | custom-call | tf_op jit(solution)/shard_map/pallas_call | solution.py:461
